TPU v7x, 32 devices: a whole 2x2x4 slice. The times are simulated.
32 devices in a mesh: pb: 2 (over y), blk: 16 (over z, x, core).
Axes of the slice: x: 2, y: 2, z: 4, core: 2. Of those that a mesh axis runs over, the one named last changes fastest.
Arguments:
- decoder_in: float32 [16, 20, 768], P('pb'), may hold values from -6 to 6
- encoded: bfloat16 [16, 16384, 768], P('pb', 'blk'), may hold values from -6 to 6
- key_ids: int32 [16, 16384], P('pb', 'blk'), may hold values 0 or 1
- buckets: int32 [20, 20], replicated, may hold values from 0 to 31
- gain_self: float32 [768], replicated, may hold values from 0.25 to 1.75
- gain_cross: float32 [768], replicated, may hold values from 0.25 to 1.75
- gain_ffn: float32 [768], replicated, may hold values from 0.25 to 1.75
- rel_bias: float32 [32, 12], replicated, may hold values from -4 to 4
- self_q: bfloat16 [768, 768], replicated, may hold values from -0.109375 to 0.109375
- self_k: bfloat16 [768, 768], replicated, may hold values from -0.109375 to 0.109375
- self_v: bfloat16 [768, 768], replicated, may hold values from -0.21875 to 0.21875
- self_o: bfloat16 [768, 768], replicated, may hold values from -0.4375 to 0.4375
- cross_q: bfloat16 [768, 768], replicated, may hold values from -0.109375 to 0.109375
- cross_k: bfloat16 [768, 768], replicated, may hold values from -0.109375 to 0.109375
- cross_v: bfloat16 [768, 768], replicated, may hold values from -0.21875 to 0.21875
- cross_o: bfloat16 [768, 768], replicated, may hold values from -1.75 to 1.75
- ffn_in: bfloat16 [768, 3072], replicated, may hold values from -0.21875 to 0.21875
- ffn_out: bfloat16 [3072, 768], replicated, may hold values from -0.15625 to 0.15625
- cotangent: float32 [16, 20, 768], P('pb'), may hold values from -6 to 6
Outputs:
- output: float32 [16, 20, 768], P('pb')
- grad_in: float32 [16, 20, 768], P('pb')
- grad_encoded: bfloat16 [16, 16384, 768], P('pb', 'blk')
- grad_gain_self: float32 [768], replicated
- grad_gain_cross: float32 [768], replicated
- grad_gain_ffn: float32 [768], replicated
- grad_rel_bias: float32 [32, 12], replicated
- grad_self_q: float32 [768, 768], P('blk')
- grad_self_k: float32 [768, 768], P('blk')
- grad_self_v: float32 [768, 768], P('blk')
- grad_self_o: float32 [768, 768], P('blk')
- grad_cross_q: float32 [768, 768], P('blk')
- grad_cross_k: float32 [768, 768], P('blk')
- grad_cross_v: float32 [768, 768], P('blk')
- grad_cross_o: float32 [768, 768], P('blk')
- grad_ffn_in: float32 [768, 3072], P('blk')
- grad_ffn_out: float32 [3072, 768], P('blk')
Inputs may be any that keep to these rules, and one draw needn't show every extreme that they name: `key_ids`: 1 marks a real encoder token, 0 a padding one.
All inputs are finite; a program needn't handle non-finite values. No bound on the sum of `key_ids` on one device may be relied on, other than what follows from the above.
Results may differ from a plain program's by a relative error of at most 0.023.
The roundings to bfloat16 on the way count: a program that leaves them out, or rounds other values in their place, can miss the bound.
Values sent between devices are 32-bit elements; how exact they have to be, the bound alone decides.
No kernel may reach another device: no remote copies, remote signals or barrier semaphores. Data moves between devices by JAX's collectives and lax.ppermute only.
A program may use at most 192 MiB of HBM per device.

v0:
```python
import jax
import jax.numpy as jnp
from jax import lax
from jax.sharding import PartitionSpec as P

EPSILON = 1e-06
MASKED = -1000000000.0
HIGHEST = lax.Precision.HIGHEST


def merged(value, axis, combine):
    everything = jax.tree.map(lambda part: lax.all_gather(part, axis), value)
    leading = jax.tree.map(lambda part: part[0], everything)

    def step(k, so_far):
        return combine(so_far, jax.tree.map(lambda part: part[k], everything))

    return lax.fori_loop(1, lax.axis_size(axis), step, leading)


def rms_norm(values, gain_vec):
    inv_scale = lax.rsqrt(jnp.mean(values * values, axis=-1, keepdims=True) + EPSILON)
    return values * inv_scale * gain_vec


def matmul(left_side, right_side):
    return jnp.dot(left_side, right_side, preferred_element_type=jnp.float32)


def matmul_nt(left_side, right_side):
    return lax.dot_general(
        left_side, right_side, (((1,), (1,)), ((), ())), preferred_element_type=jnp.float32
    )


def matmul_tn(left_side, right_side):
    return lax.dot_general(
        left_side, right_side, (((0,), (0,)), ((), ())), preferred_element_type=jnp.float32
    )


def exact_mm(left_side, right_side):
    return jnp.dot(left_side, right_side.astype(jnp.float32), precision=HIGHEST)


def exact_nt(left_side, right_side):
    return lax.dot_general(
        left_side, right_side.astype(jnp.float32), (((1,), (1,)), ((), ())), precision=HIGHEST
    )


def exact_tn(left_side, right_side):
    return lax.dot_general(
        left_side.astype(jnp.float32),
        right_side.astype(jnp.float32),
        (((0,), (0,)), ((), ())),
        precision=HIGHEST,
    )


def columns(values, blk_index, share):
    return lax.dynamic_slice_in_dim(values, blk_index * share, share, 1)


def combine_stats(earlier, later):
    maximum = jnp.maximum(earlier[0], later[0])
    return (
        maximum,
        earlier[1] * jnp.exp(earlier[0] - maximum) + later[1] * jnp.exp(later[0] - maximum),
    )


def body(
    decoder_in,
    encoded,
    key_ids,
    buckets,
    gain_self,
    gain_cross,
    gain_ffn,
    rel_bias,
    self_q,
    self_k,
    self_v,
    self_o,
    cross_q,
    cross_k,
    cross_v,
    cross_o,
    ffn_in,
    ffn_out,
    cotangent,
):
    low_type = jnp.bfloat16
    questions, answer_len, features = decoder_in.shape
    enc_rows = encoded.shape[1]
    head_count = rel_bias.shape[1]
    head_size = features // head_count
    hidden_units = ffn_in.shape[1]
    blk_count = lax.axis_size("blk")
    blk_index = lax.axis_index("blk")
    row_count = questions * answer_len
    feature_share = features // blk_count
    hidden_share = hidden_units // blk_count
    flat_in = decoder_in.reshape(row_count, features)
    norm_one, norm_one_back = jax.vjp(rms_norm, flat_in, gain_self)
    normed_one = norm_one.astype(low_type)
    self_weights = jnp.concatenate([self_q, self_k, self_v], axis=1)
    projected = matmul(normed_one, self_weights).astype(low_type)
    projected = projected.reshape(questions, answer_len, 3, head_count, head_size)
    query_self = projected[:, :, 0]
    key_self = projected[:, :, 1]
    value_self = projected[:, :, 2]
    bucket_hot = (buckets[:, :, None] == jnp.arange(rel_bias.shape[0], dtype=jnp.int32)).astype(
        jnp.float32
    )
    position_bias = jnp.einsum("ijb,bh->hij", bucket_hot, rel_bias, precision=HIGHEST)
    positions = jnp.arange(answer_len)
    causal = jnp.where(positions[None, :] <= positions[:, None], 0.0, MASKED)
    raw_self = jnp.einsum(
        "qihd,qjhd->qhij", query_self, key_self, preferred_element_type=jnp.float32
    )
    probs_self = jax.nn.softmax(raw_self + position_bias + causal, axis=-1)
    probs_self_low = probs_self.astype(low_type)
    context_self = jnp.einsum(
        "qhij,qjhd->qihd", probs_self_low, value_self, preferred_element_type=jnp.float32
    )
    context_self = context_self.reshape(row_count, features).astype(low_type)
    after_self = flat_in + matmul(context_self, self_o)
    norm_two, norm_two_back = jax.vjp(rms_norm, after_self, gain_cross)
    normed_two = norm_two.astype(low_type)
    query_cross = (
        matmul(normed_two, cross_q)
        .astype(low_type)
        .reshape(questions, answer_len, head_count, head_size)
    )
    flat_enc = encoded.reshape(questions * enc_rows, features)
    kv_weights = jnp.concatenate([cross_k, cross_v], axis=1)
    kv_cross = (
        matmul(flat_enc, kv_weights)
        .astype(low_type)
        .reshape(questions, enc_rows, 2, head_count, head_size)
    )
    key_cross = kv_cross[:, :, 0]
    value_cross = kv_cross[:, :, 1]
    key_mask = jnp.where(key_ids != 0, 0.0, MASKED)[:, None, None, :]

    def cross_scores():
        raw_cross = jnp.einsum(
            "qihd,qjhd->qhij", query_cross, key_cross, preferred_element_type=jnp.float32
        )
        return raw_cross + key_mask

    scores = cross_scores()
    local_top = jnp.max(scores, axis=-1)
    local_total = jnp.sum(jnp.exp(scores - local_top[..., None]), axis=-1)
    maximum, normalizer = merged((local_top, local_total), "blk", combine_stats)
    probs_cross = jnp.exp(scores - maximum[..., None]) / normalizer[..., None]
    partial_context = jnp.einsum(
        "qhij,qjhd->qihd",
        probs_cross.astype(low_type),
        value_cross,
        preferred_element_type=jnp.float32,
    )
    context_full = lax.psum(partial_context, "blk")
    context_cross = context_full.reshape(row_count, features)
    after_cross = after_self + exact_mm(context_cross, cross_o)
    norm_three, norm_three_back = jax.vjp(rms_norm, after_cross, gain_ffn)
    normed_three = norm_three.astype(low_type)
    ffn_inner = matmul(normed_three, ffn_in)
    active, active_back = jax.vjp(jax.nn.gelu, ffn_inner)
    active_low = active.astype(low_type)
    output = after_cross + matmul(active_low, ffn_out)
    grad_out = cotangent.reshape(row_count, features)
    grad_out_low = grad_out.astype(low_type)
    grad_active = matmul_nt(grad_out_low, ffn_out).astype(low_type)
    grad_inner = active_back(grad_active.astype(jnp.float32))[0].astype(low_type)
    back_three, grad_gain_ffn = norm_three_back(matmul_nt(grad_inner, ffn_in))
    grad_after_cross = grad_out + back_three
    grad_ffn_out = matmul_tn(columns(active_low, blk_index, hidden_share), grad_out_low)
    grad_ffn_in = matmul_tn(columns(normed_three, blk_index, feature_share), grad_inner)
    grad_branch_cross = grad_after_cross.astype(low_type)
    grad_cross_o = exact_tn(columns(context_cross, blk_index, feature_share), grad_branch_cross)
    grad_context_cross = matmul_nt(grad_branch_cross, cross_o).astype(low_type)
    grad_context_cross = grad_context_cross.reshape(questions, answer_len, head_count, head_size)
    scores = cross_scores()
    probs_cross = jnp.exp(scores - maximum[..., None]) / normalizer[..., None]
    grad_probs = jnp.einsum(
        "qihd,qjhd->qhij", grad_context_cross, value_cross, preferred_element_type=jnp.float32
    )
    delta = lax.psum(jnp.sum(probs_cross * grad_probs, axis=-1), "blk")
    grad_scores_cross = (probs_cross * (grad_probs - delta[..., None])).astype(low_type)
    grad_value_cross = jnp.einsum(
        "qhij,qihd->qjhd",
        probs_cross.astype(low_type),
        grad_context_cross,
        preferred_element_type=jnp.float32,
    ).astype(low_type)
    grad_key_cross = jnp.einsum(
        "qhij,qihd->qjhd", grad_scores_cross, query_cross, preferred_element_type=jnp.float32
    ).astype(low_type)
    partial_query = jnp.einsum(
        "qhij,qjhd->qihd", grad_scores_cross, key_cross, preferred_element_type=jnp.float32
    )
    grad_query_cross = lax.psum(partial_query, "blk")
    grad_query_cross = grad_query_cross.reshape(row_count, features)
    grad_kv = jnp.concatenate(
        [
            grad_key_cross.reshape(questions * enc_rows, features),
            grad_value_cross.reshape(questions * enc_rows, features),
        ],
        axis=1,
    )
    grad_encoded = (
        matmul_nt(grad_kv, kv_weights).reshape(questions, enc_rows, features).astype(low_type)
    )
    whole_sum = lax.psum(matmul_tn(flat_enc, grad_kv), "blk")
    kv_grad_share = lax.dynamic_slice_in_dim(whole_sum, blk_index * feature_share, feature_share, 0)
    grad_cross_q = exact_tn(columns(normed_two, blk_index, feature_share), grad_query_cross)
    back_two, grad_gain_cross = norm_two_back(exact_nt(grad_query_cross, cross_q))
    grad_after_self = grad_after_cross + back_two
    grad_branch_self = grad_after_self.astype(low_type)
    grad_self_o = matmul_tn(columns(context_self, blk_index, feature_share), grad_branch_self)
    grad_context_self = matmul_nt(grad_branch_self, self_o).astype(low_type)
    grad_context_self = grad_context_self.reshape(questions, answer_len, head_count, head_size)
    grad_probs_self = jnp.einsum(
        "qihd,qjhd->qhij", grad_context_self, value_self, preferred_element_type=jnp.float32
    )
    grad_scores_self = probs_self * (
        grad_probs_self - jnp.sum(probs_self * grad_probs_self, axis=-1, keepdims=True)
    )
    grad_bias = jnp.einsum("qhij,ijb->bh", grad_scores_self, bucket_hot, precision=HIGHEST)
    grad_scores_low = grad_scores_self.astype(low_type)
    grad_query_self = jnp.einsum(
        "qhij,qjhd->qihd", grad_scores_low, key_self, preferred_element_type=jnp.float32
    )
    grad_key_self = jnp.einsum(
        "qhij,qihd->qjhd", grad_scores_low, query_self, preferred_element_type=jnp.float32
    )
    grad_value_self = jnp.einsum(
        "qhij,qihd->qjhd", probs_self_low, grad_context_self, preferred_element_type=jnp.float32
    )
    grad_qkv = jnp.stack([grad_query_self, grad_key_self, grad_value_self], axis=2).astype(low_type)
    grad_qkv = grad_qkv.reshape(row_count, 3 * features)
    back_one, grad_gain_self = norm_one_back(matmul_nt(grad_qkv, self_weights))
    grad_in = grad_after_self + back_one
    grad_self_qkv = matmul_tn(columns(normed_one, blk_index, feature_share), grad_qkv)
    summed = lax.psum(
        (
            grad_self_qkv,
            grad_self_o,
            grad_cross_q,
            kv_grad_share,
            grad_cross_o,
            grad_ffn_in,
            grad_ffn_out,
            grad_gain_self,
            grad_gain_cross,
            grad_gain_ffn,
            grad_bias,
        ),
        "pb",
    )
    self_qkv_sum = summed[0]
    kv_sum = summed[3]
    return (
        output.reshape(questions, answer_len, features),
        grad_in.reshape(questions, answer_len, features),
        grad_encoded,
        summed[7],
        summed[8],
        summed[9],
        summed[10],
        self_qkv_sum[:, :features],
        self_qkv_sum[:, features : 2 * features],
        self_qkv_sum[:, 2 * features :],
        summed[1],
        summed[2],
        kv_sum[:, :features],
        kv_sum[:, features:],
        summed[4],
        summed[5],
        summed[6],
    )


def solution(mesh):
    placed = (
        P("pb", None, None),
        P("pb", "blk", None),
        P("pb", "blk"),
        P(),
        P(),
        P(),
        P(),
        P(),
        P(),
        P(),
        P(),
        P(),
        P(),
        P(),
        P(),
        P(),
        P(),
        P(),
        P("pb", None, None),
    )
    return jax.shard_map(
        body,
        mesh=mesh,
        in_specs=placed,
        out_specs=(
            P("pb", None, None),
            P("pb", None, None),
            P("pb", "blk", None),
            P(),
            P(),
            P(),
            P(),
            P("blk", None),
            P("blk", None),
            P("blk", None),
            P("blk", None),
            P("blk", None),
            P("blk", None),
            P("blk", None),
            P("blk", None),
            P("blk", None),
            P("blk", None),
        ),
        check_vma=False,
    )
```

profile of v0, /device:TPU:0, one launch (start us, length us, event | category | flops | bytes accessed | tf_op | source)
XLA Modules:
  0.0 784.7 jit_solution(2897254566395547427)
XLA Ops:
  12.4 2.6 constant_dynamic-update-slice_fusion.4
  20.4 2.1 reshape.175
  22.6 2.7 fusion.73
  28.2 2.1 fusion.24
  31.2 2.2 convert_element_type.103
  39.8 25.8 %convolution_convert_fusion = bf16[1536,8192]{1,0:T(8,128)(2,1)} fusion(bf16[768,1536]{1,0:T(8,128)(2,1)} %constant_dynamic-update-slice_fusion.3, bf16[8192,768]{1,0:T(8,128)(2,1)} %bitcast.150), kind=kOutput, calls=%fused_computation.6 | convolution fusion | flops 19339935744 | bytes 40108032 | tf_op jit(solution)/shard_map/dot_general | solution.py:27
  65.6 22.7 %copy.238 = bf16[192,8,8,1024]{3,2,1,0:T(8,128)(2,1)S(1)} copy(bf16[192,8,8,1024]{3,1,2,0:T(8,128)(2,1)} %bitcast.145) | data formatting | bytes 50331648
  88.3 8.9 %fusion.72 = (bf16[8,1024,1,12,64]{1,0,4,3,2:T(8,128)(2,1)}, bf16[8,1024,1,12,64]{1,0,4,3,2:T(8,128)(2,1)}) fusion(bf16[8,1024,2,12,64]{1,0,4,3,2:T(8,128)(2,1)S(1)} %bitcast.138), kind=kLoop, calls=%fused_computation.142 | loop fusion | bytes 50331648 | tf_op jit(solution)/shard_map/slice | solution.py:144
  97.2 22.4 %add_reduce_fusion = (f32[8,12,20]{2,1,0:T(8,128)S(1)}, f32[8,12,20,1024]{3,2,1,0:T(8,128)S(1)}) fusion(f32[8,1024]{1,0:T(8,128)S(1)} %compare_select_fusion, bf16[8,1024,1,12,64]{1,0,4,3,2:T(8,128)(2,1)} %get-tuple-element.310, bf16[8,20,12,64]{3,2,1,0:T(8,128)(2,1)S(1)} %reshape.178), kind=kOutput, calls=%fused_computation.20 | convolution fusion | flops 255588480 | bytes 20733440 | tf_op jit(solution)/shard_map/qihd,qjhd->qhij/dot_general | solution.py:149
  119.7 2.1 exponential_reduce_fusion
  123.2 25.4 %all-gather.1 = f32[128,12,20]{2,0,1:T(8,128)S(1)} all-gather(f32[8,12,20]{2,0,1:T(8,128)S(1)} %copy.207), channel_id=3, replica_groups=mesh['pb'=2,'blk'=16] {'blk'}, dimensions={0}, use_global_device_ids=true | all-gather | bytes 130560 | tf_op jit(solution)/shard_map/all_gather | solution.py:12
  148.7 19.6 %all-gather = f32[128,12,20]{2,0,1:T(8,128)S(1)} all-gather(f32[8,12,20]{2,0,1:T(8,128)S(1)} %copy.206), channel_id=2, replica_groups=mesh['pb'=2,'blk'=16] {'blk'}, dimensions={0}, use_global_device_ids=true | all-gather | bytes 130560 | tf_op jit(solution)/shard_map/all_gather | solution.py:12
  169.2 13.5 %while.17 = (s32[]{:T(128)}, f32[8,12,20]{2,0,1:T(8,128)S(1)}, f32[8,12,20]{2,0,1:T(8,128)S(1)}, f32[16,8,12,20]{3,1,0,2:T(8,128)}, f32[16,8,12,20]{3,1,0,2:T(8,128)S(1)}, /*index=5*/s32[]{:T(128)}, s32[]{:T(128)}, s32[]{:T(128)}) while((s32[]{:T(128)}, f32[8,12,20]{2,0,1:T(8,128)S(1)}, f32[8,12,20]{2,0,1:T(8,128)S(1)}, ...), condition=%wide.region_7.8_spmd, body=%wide.region_6.7_spmd.sunk | while | flops 11525 | bytes 46203 | solution.py:18
  183.3 23.2 %fusion.19 = f32[8,20,12,64]{3,1,2,0:T(8,128)S(1)} fusion(bf16[8,1024,1,12,64]{1,0,4,3,2:T(8,128)(2,1)} %get-tuple-element.311, f32[8,12,20,1024]{3,2,1,0:T(8,128)} %copy-done.1, f32[8,12,20]{2,1,0:T(8,128)S(1)} %copy.211, f32[8,12,20]{2,1,0:T(8,128)S(1)} %copy.210, f32[8,1024]{1,0:T(8,128)S(1)} %compare_select_fusion), kind=kOutput, calls=%fused_computation.40 | convolution fusion | flops 259522560 | bytes 20986880 | tf_op jit(solution)/shard_map/qhij,qjhd->qihd/dot_general | solution.py:159
  207.9 2.4 reshape.179
  214.3 85.9 %all-reduce.7.cloned.1.call-done = f32[160,768]{1,0:T(8,128)} async-done(((f32[160,768]{1,0:T(8,128)}), f32[160,768]{1,0:T(8,128)}) %all-reduce.7.cloned.1.call-update) | async-done | bytes 491536 | tf_op jit(solution)/shard_map/psum | solution.py:165
  302.3 4.8 multiply_convert_fusion.1
  307.1 4.5 fusion.16
  311.7 2.5 multiply_reduce_fusion.2
  315.6 2.2 reshape.182
  317.8 21.2 %multiply_reduce_fusion = (f32[8,12,20]{2,1,0:T(8,128)}, f32[8,12,20,1024]{3,2,1,0:T(8,128)}) fusion(f32[8,12,20]{2,1,0:T(8,128)S(1)} %copy-done.34, f32[8,12,20]{2,1,0:T(8,128)S(1)} %copy-done.36, f32[8,12,20,1024]{3,2,1,0:T(8,128)} %copy-done.1, f32[8,1024]{1,0:T(8,128)S(1)} %compare_select_fusion, bf16[8,1024,1,12,64]{1,0,4,3,2:T(8,128)(2,1)} %get-tuple-element.311, ...), kind=kOutput, calls=%fused_computation.17 | convolution fusion | flops 261486720 | bytes 28613120 | tf_op jit(solution)/shard_map/qihd,qjhd->qhij/dot_general | solution.py:188
  338.9 12.0 %convert_bitcast_fusion = bf16[8,1024,12,64]{1,3,2,0:T(8,128)(2,1)} fusion(bf16[8,20,12,64]{3,2,1,0:T(8,128)(2,1)} %reshape.182, f32[8,12,20,1024]{3,2,1,0:T(8,128)} %copy-done.1, f32[8,12,20]{2,1,0:T(8,128)S(1)} %copy-done.34, f32[8,12,20]{2,1,0:T(8,128)S(1)} %copy-done.36, f32[8,1024]{1,0:T(8,128)S(1)} %compare_select_fusion), kind=kOutput, calls=%fused_computation.10 | convolution fusion | flops 265814016 | bytes 20741120 | tf_op jit(solution)/shard_map/qhij,qihd->qjhd/dot_general | solution.py:193
  350.9 59.1 %psum.106 = f32[8,12,20]{2,1,0:T(8,128)S(1)} all-reduce(f32[8,12,20]{2,1,0:T(8,128)} %get-tuple-element.333), channel_id=1, replica_groups=mesh['pb'=2,'blk'=16] {'blk'}, use_global_device_ids=true, to_apply=%region_12.13 | all-reduce | flops 1920 | bytes 15360 | tf_op jit(solution)/shard_map/psum | solution.py:191
  410.1 10.1 %multiply_convert_fusion = bf16[8,12,20,1024]{3,2,1,0:T(8,128)(2,1)} fusion(f32[8,12,20,1024]{3,2,1,0:T(8,128)} %get-tuple-element.334, f32[8,12,20]{2,1,0:T(8,128)S(1)} %psum.106, f32[8,12,20]{2,1,0:T(8,128)S(1)} %copy-done.34, f32[8,12,20]{2,1,0:T(8,128)S(1)} %copy-done.36, f32[8,12,20,1024]{3,2,1,0:T(8,128)} %copy-done.1, f32[8,1024]{1,0:T(8,128)S(1)} %compare_select_fusion), kind=kLoop, calls=%fused_computation.16 | loop fusion | flops 11796480 | bytes 19716608 | tf_op jit(solution)/shard_map/convert_element_type | solution.py:192
  420.2 21.6 %fusion.22 = f32[8,20,12,64]{3,1,2,0:T(8,128)} fusion(bf16[8,12,20,1024]{3,2,1,0:T(8,128)(2,1)} %multiply_convert_fusion, bf16[8,1024,1,12,64]{1,0,4,3,2:T(8,128)(2,1)} %get-tuple-element.310), kind=kOutput, calls=%fused_computation.41 | convolution fusion | flops 251658240 | bytes 17006592 | tf_op jit(solution)/shard_map/qhij,qjhd->qihd/dot_general | solution.py:202
  441.8 10.7 %convert_bitcast_fusion.1 = bf16[8,1024,12,64]{1,3,2,0:T(8,128)(2,1)} fusion(bf16[8,12,20,1024]{3,2,1,0:T(8,128)(2,1)} %multiply_convert_fusion, bf16[8,20,12,64]{3,2,1,0:T(8,128)(2,1)S(1)} %reshape.178), kind=kOutput, calls=%fused_computation.11 | convolution fusion | flops 257949696 | bytes 16760832 | tf_op jit(solution)/shard_map/qhij,qihd->qjhd/dot_general | solution.py:199
  453.8 2.4 reshape.183
  456.2 12.3 %copy.223 = bf16[8,1024,12,64]{1,0,3,2:T(8,128)(2,1)S(1)} copy(bf16[8,1024,12,64]{1,3,2,0:T(8,128)(2,1)} %convert_bitcast_fusion) | data formatting | bytes 25165824 | tf_op jit(solution)/shard_map/convert_element_type | solution.py:198
  468.5 7.9 %copy.240 = bf16[96,8,8,1024]{3,1,2,0:T(8,128)(2,1)S(1)} copy(bf16[96,8,8,1024]{3,2,1,0:T(8,128)(2,1)S(1)} %bitcast.142) | data formatting | bytes 25165824
  476.4 22.0 %copy.221 = bf16[8,1024,12,64]{1,0,3,2:T(8,128)(2,1)S(1)} copy(bf16[8,1024,12,64]{1,3,2,0:T(8,128)(2,1)S(1)} %bitcast.140) | data formatting | bytes 25165824 | tf_op jit(solution)/shard_map/convert_element_type | solution.py:201
  498.4 7.9 %copy.239 = bf16[96,8,8,1024]{3,1,2,0:T(8,128)(2,1)S(1)} copy(bf16[96,8,8,1024]{3,2,1,0:T(8,128)(2,1)S(1)} %bitcast.143) | data formatting | bytes 25165824
  506.3 6.3 constant_dynamic-update-slice_fusion.6
  512.6 5.9 constant_dynamic-update-slice_fusion.5
  518.9 24.9 %convolution_bitcast_fusion = f32[768,1536]{0,1:T(8,128)} fusion(bf16[8192,1536]{0,1:T(8,128)(2,1)} %constant_dynamic-update-slice_fusion.5, bf16[8192,768]{1,0:T(8,128)(2,1)S(1)} %bitcast.153), kind=kOutput, calls=%fused_computation.21 | convolution fusion | flops 19327352832 | bytes 42467328 | tf_op jit(solution)/shard_map/dot_general | solution.py:37
  545.9 2.1 fusion.48
  548.0 2.5 fusion.55
  550.5 115.0 %all-reduce.9.cloned.1.call-done = (f32[160,768]{1,0:T(8,128)}, f32[768,1536]{0,1:T(8,128)}) async-done(((f32[160,768]{1,0:T(8,128)}, f32[768,1536]{0,1:T(8,128)}), (f32[160,768]{1,0:T(8,128)}, f32[768,1536]{0,1:T(8,128)})) %all-reduce.9.cloned.1.call-update) | async-done | bytes 5210128 | tf_op jit(solution)/shard_map/psum | solution.py:205
  665.5 2.1 fusion.57
  667.7 2.5 multiply_reduce_fusion.3
  675.5 2.0 fusion.27
  680.2 2.6 constant_dynamic-slice_fusion
  683.6 2.2 convert_element_type.121
  685.8 2.4 fusion.60
  688.3 26.5 %convolution_convert_fusion.1 = bf16[8192,768]{1,0:T(8,128)(2,1)} fusion(bf16[8192,1536]{0,1:T(8,128)(2,1)} %constant_dynamic-update-slice_fusion.5, bf16[768,1536]{1,0:T(8,128)(2,1)S(1)} %copy-done.29), kind=kOutput, calls=%fused_computation.7 | convolution fusion | flops 19333644288 | bytes 40108032 | tf_op jit(solution)/shard_map/dot_general | solution.py:31
  714.8 3.4 convolution_add_fusion.3
  720.4 3.5 multiply_reduce_fusion.4
  725.4 8.9 %all-reduce.1 = (f32[768]{0:T(1024)}, f32[768]{0:T(1024)}, f32[768]{0:T(1024)}, f32[32,12]{0,1:T(8,128)}) all-reduce(f32[768]{0:T(1024)S(1)} %get-tuple-element.283, f32[768]{0:T(1024)S(1)} %get-tuple-element.281, f32[768]{0:T(1024)S(1)} %copy-done.50, ...), channel_id=1, replica_groups=mesh['pb'=2,'blk'=16] {'pb'}, use_global_device_ids=true, to_apply=%region_18.19 | all-reduce | flops 2688 | bytes 21504 | tf_op jit(solution)/shard_map/psum | solution.py:248
  734.3 34.4 %all-reduce.11.cloned.1.call-done = (f32[48,2304]{1,0:T(8,128)}, f32[48,768]{1,0:T(8,128)}, f32[48,768]{1,0:T(8,128)}, f32[48,1536]{0,1:T(8,128)}, f32[48,768]{1...) async-done(((f32[48,2304]{1,0:T(8,128)}, f32[48,768]{1,0:T(8,128)}, f32[48,768]{1,0:T(8,128)}, f32[48,1536]{0,1:T(8,128)}, f32[48,768]{1,0:T(8,128)}, ...) | async-done | bytes 2359312 | tf_op jit(solution)/shard_map/psum | solution.py:248
  (221 shorter events, 70.5 us)
Async XLA Ops:
  7.2 29.0 %copy-start = (bf16[768,768]{1,0:T(8,128)(2,1)S(1)}, bf16[768,768]{1,0:T(8,128)(2,1)}, u32[]{:S(2)}) copy-start(bf16[768,768]{1,0:T(8,128)(2,1)} %param.33) | copy-start | bytes 3538948
  7.2 293.0 %all-reduce.7.cloned.1.call-start = ((), (), s32[]{:S(2)}) async-start(), calls=%async_computation | async-start | bytes 983040 | tf_op jit(solution)/shard_map/psum | solution.py:165
  9.9 7.9 %copy-start.53 = (f32[160]{0:T(256)}, f32[160]{0:T(256)S(1)}, u32[]{:S(2)}) copy-start(f32[160]{0:T(256)S(1)} %add.172) | copy-start | bytes 1924
  9.9 8.0 %copy-start.46 = (f32[160]{0:T(256)}, f32[160]{0:T(256)S(1)}, u32[]{:S(2)}) copy-start(f32[160]{0:T(256)S(1)} %rsqrt.30) | copy-start | bytes 1924
  12.4 21.1 %copy-start.5 = (f32[160,768]{1,0:T(8,128)}, f32[160,768]{1,0:T(8,128)S(1)}, u32[]{:S(2)}) copy-start(f32[160,768]{1,0:T(8,128)S(1)} %reshape.174) | copy-start | bytes 1474564
  12.4 5.4 copy-start.21
  28.2 5.3 copy-start.12
  28.2 6.8 copy-start.42
  34.9 3.7 copy-start.22
  119.6 3.6 copy-start.1
  206.6 93.7 %copy-start.10 = (bf16[768,768]{1,0:T(8,128)(2,1)S(1)}, bf16[768,768]{1,0:T(8,128)(2,1)}, u32[]{:S(2)}) copy-start(bf16[768,768]{1,0:T(8,128)(2,1)} %param.36) | copy-start | bytes 3538948
  207.9 94.3 %copy-start.41 = (f32[768]{0:T(1024)S(1)}, f32[768]{0:T(1024)}, u32[]{:S(2)}) copy-start(f32[768]{0:T(1024)} %param.27) | copy-start | bytes 9220
  210.3 455.2 %all-reduce.9.cloned.1.call-start = ((), (), s32[]{:S(2)}) async-start(), calls=%async_computation.1 | async-start | bytes 10420224 | tf_op jit(solution)/shard_map/psum | solution.py:205
  302.1 12.0 %copy-start.3 = (f32[160,768]{1,0:T(8,128)}, f32[160,768]{1,0:T(8,128)S(1)}, u32[]{:S(2)}) copy-start(f32[160,768]{1,0:T(8,128)S(1)} %get-tuple-element.329) | copy-start | bytes 1474564
  302.3 4.8 copy-start.32
  302.3 4.8 copy-start.13
  302.3 9.3 %slice-start.3 = ((s8[4718592]{0:T(1024)(128)(4,1)}), s8[4194304]{0:T(1024)(128)(4,1)S(1)}, s32[]{:S(2)}) async-start(s8[4718592]{0:T(1024)(128)(4,1)} %bitcast.146), calls=%async_computation.6 | async-start | bytes 8388608
  307.1 4.5 slice-start.4
  314.1 3.7 copy-start.34
  314.1 3.7 copy-start.36
  441.8 10.7 %copy-start.23 = (f32[8,20,12,64]{3,1,2,0:T(8,128)S(1)}, f32[8,20,12,64]{3,1,2,0:T(8,128)}, u32[]{:S(2)}) copy-start(f32[8,20,12,64]{3,1,2,0:T(8,128)} %fusion.22) | copy-start | bytes 1474564
  456.2 20.2 %slice-start = ((s8[12582912]{0:T(1024)(128)(4,1)}), s8[4194304]{0:T(1024)(128)(4,1)S(1)}, s32[]{:S(2)}) async-start(s8[12582912]{0:T(1024)(128)(4,1)} %bitcast.139), calls=%async_computation.3 | async-start | bytes 8388608
  456.2 20.2 %slice-start.1 = ((s8[12582912]{0:T(1024)(128)(4,1)}), s8[4194304]{0:T(1024)(128)(4,1)S(1)}, s32[]{:S(2)}) async-start(s8[12582912]{0:T(1024)(128)(4,1)} %bitcast.139), calls=%async_computation.4 | async-start | bytes 8388608
  468.5 7.9 %slice-start.2 = ((s8[12582912]{0:T(1024)(128)(4,1)}), s8[4194304]{0:T(1024)(128)(4,1)S(1)}, s32[]{:S(2)}) async-start(s8[12582912]{0:T(1024)(128)(4,1)} %bitcast.139), calls=%async_computation.5 | async-start | bytes 8388608
  506.3 12.2 %slice-start.5 = ((s8[12582912]{0:T(1024)(128)(4,1)}), s8[4194304]{0:T(1024)(128)(4,1)S(1)}, s32[]{:S(2)}) async-start(s8[12582912]{0:T(1024)(128)(4,1)} %bitcast.151), calls=%async_computation.8 | async-start | bytes 8388608
  506.3 12.2 %slice-start.6 = ((s8[12582912]{0:T(1024)(128)(4,1)}), s8[4194304]{0:T(1024)(128)(4,1)S(1)}, s32[]{:S(2)}) async-start(s8[12582912]{0:T(1024)(128)(4,1)} %bitcast.151), calls=%async_computation.9 | async-start | bytes 8388608
  512.6 6.4 slice-start.7
  543.8 123.8 %copy-start.43 = (f32[768]{0:T(1024)S(1)}, f32[768]{0:T(1024)}, u32[]{:S(2)}) copy-start(f32[768]{0:T(1024)} %param.26) | copy-start | bytes 9220
  543.8 123.8 %copy-start.49 = (f32[160]{0:T(256)S(1)}, f32[160]{0:T(256)}, u32[]{:S(2)}) copy-start(f32[160]{0:T(256)} %copy-done.48) | copy-start | bytes 1924
  543.9 126.3 %copy-start.52 = (f32[160]{0:T(256)S(1)}, f32[160]{0:T(256)}, u32[]{:S(2)}) copy-start(f32[160]{0:T(256)} %copy-done.51) | copy-start | bytes 1924
  543.9 224.8 %all-reduce.11.cloned.1.call-start = ((), (), s32[]{:S(2)}) async-start(), calls=%async_computation.2 | async-start | bytes 5701632 | tf_op jit(solution)/shard_map/psum | solution.py:248
  667.6 7.8 copy-start.40
  670.3 7.2 copy-start.7
  672.3 5.2 copy-start.20
  688.2 26.5 %copy-start.4 = (f32[160,768]{1,0:T(8,128)S(1)}, f32[160,768]{1,0:T(8,128)}, u32[]{:S(2)}) copy-start(f32[160,768]{1,0:T(8,128)} %copy-done.3) | copy-start | bytes 1474564
  688.3 26.5 %copy-start.24 = (bf16[160,3072]{1,0:T(8,128)(2,1)S(1)}, bf16[160,3072]{1,0:T(8,128)(2,1)}, u32[]{:S(2)}) copy-start(bf16[160,3072]{1,0:T(8,128)(2,1)} %get-tuple-element.330) | copy-start | bytes 2949124
  714.8 5.5 copy-start.6
  714.8 5.5 copy-start.9
  714.8 5.5 copy-start.45
  714.8 5.5 copy-start.47
  718.2 5.6 copy-start.54
  718.3 5.6 copy-start.8
  720.3 4.7 copy-start.55
  720.3 5.1 copy-start.50
  768.7 6.3 copy-start.38
  768.7 7.0 copy-start.37
  768.7 7.6 copy-start.31
  768.7 8.4 %copy-start.30 = (f32[192,768]{1,0:T(8,128)S(1)}, f32[192,768]{1,0:T(8,128)}, u32[]{:S(2)}) copy-start(f32[192,768]{1,0:T(8,128)} %get-tuple-element.414) | copy-start | bytes 1769476
  (19 other events, 29.5 us)
Sparse Core Ops, SparseCore 0:
  210.5 89.7 all-reduce.6
  544.0 121.4 all-reduce.8
  688.4 80.3 all-reduce.10
where the time goes:
time: 800 us; the launch traced here: 785 us
  matrix products  240 us (30%)
  waiting for transfers between devices  235 us (29%)
  local copies, waits for them, and re-layouts  151 us (19%)
  blocking collectives  113 us (14%)
  other arithmetic  29.5 us (4%)
  between operations  14.9 us (2%)
    psum x1, waiting for transfers between devices, body(): grad_query_cross = lax.psum(partial_query, 'blk')  115 us
    psum x1, waiting for transfers between devices, body(): context_full = lax.psum(partial_context, 'blk')  85.9 us
    unnamed x146, local copies, waits for them, and re-layouts  68.8 us
    psum x1, blocking collectives, body(): delta = lax.psum(jnp.sum(probs_cross * grad_probs, axis=-1), 'blk')  59.1 us
    all_gather x2, blocking collectives, merged(): everything = jax.tree.map(lambda part: lax.all_gather(part, axis), value)  45 us
    dot_general x6, matrix products, matmul_nt(): lax.dot_general(left_side, right_side, (((1,), (1,)), ((), ())), preferre...  40.1 us
    dot_general x6, matrix products, matmul(): return jnp.dot(left_side, right_side, preferred_element_type=jnp.float32)  37.2 us
    psum x1, waiting for transfers between devices, body(): lax.psum((grad_self_qkv, grad_self_o, grad_cross_q, kv_grad_share, grad_c...  34.4 us
  transfers between devices with their start and end apart: 3, of which 3 were waited for; matrix products, arithmetic and copies ran while one was open for 6% of the time, Pallas kernels for 0%

commit v1 on v0

--- a/solution.py
+++ b/solution.py
@@ -1,21 +1,250 @@
+import functools
+
 import jax
 import jax.numpy as jnp
 from jax import lax
+from jax.experimental import pallas as pl
+from jax.experimental.pallas import tpu as pltpu
 from jax.sharding import PartitionSpec as P
 
 EPSILON = 1e-06
 MASKED = -1000000000.0
 HIGHEST = lax.Precision.HIGHEST
 
-
-def merged(value, axis, combine):
-    everything = jax.tree.map(lambda part: lax.all_gather(part, axis), value)
-    leading = jax.tree.map(lambda part: part[0], everything)
-
-    def step(k, so_far):
-        return combine(so_far, jax.tree.map(lambda part: part[k], everything))
-
-    return lax.fori_loop(1, lax.axis_size(axis), step, leading)
+HEAD = 64
+GROUP = 4
+WIDE = GROUP * HEAD
+LANES = 128
+
+
+def nt(a, b):
+    return lax.dot_general(a, b, (((1,), (1,)), ((), ())), preferred_element_type=jnp.float32)
+
+
+def nn(a, b):
+    return jnp.dot(a, b, preferred_element_type=jnp.float32)
+
+
+def tn(a, b):
+    return lax.dot_general(a, b, (((0,), (0,)), ((), ())), preferred_element_type=jnp.float32)
+
+
+def row_head(ans, width):
+    row = lax.broadcasted_iota(jnp.int32, (GROUP * ans, width), 0)
+    head = jnp.zeros_like(row)
+    for k in range(1, GROUP):
+        head = head + (row >= k * ans).astype(jnp.int32)
+    return head
+
+
+def own_columns(ans):
+    col = lax.broadcasted_iota(jnp.int32, (GROUP * ans, WIDE), 1)
+    return (col // HEAD) == row_head(ans, WIDE)
+
+
+def own_lane(ans, group, first=0):
+    col = lax.broadcasted_iota(jnp.int32, (GROUP * ans, LANES), 1)
+    return col == row_head(ans, LANES) + (group * GROUP + first)
+
+
+def fold(block, ans):
+    half = block[: 2 * ans] + block[2 * ans :]
+    return half[:ans] + half[ans:]
+
+
+def spread(rows):
+    twice = jnp.concatenate([rows, rows], axis=0)
+    return jnp.concatenate([twice, twice], axis=0)
+
+
+def block_diagonal(values_ref, dest_ref, questions, ans, groups):
+    own = own_columns(ans)
+    per = GROUP * ans
+    for q in range(questions):
+        rows = spread(values_ref[q * ans : (q + 1) * ans, :])
+        for g in range(groups):
+            part = jnp.where(own, rows[:, g * WIDE : (g + 1) * WIDE], 0.0)
+            dest_ref[g, q * per : (q + 1) * per, :] = part.astype(jnp.bfloat16)
+
+
+def absorb(bd_ref, weight_ref, dest_ref, questions, ans, groups):
+    per = GROUP * ans
+    for g in range(groups):
+        got = nt(bd_ref[g], weight_ref[:, g * WIDE : (g + 1) * WIDE]).astype(jnp.bfloat16)
+        for q in range(questions):
+            dest_ref[q, g * per : (g + 1) * per, :] = got[q * per : (q + 1) * per]
+
+
+def project_heads(wide_ref, weight_ref, dest_ref, questions, ans, groups):
+    own = own_columns(ans)
+    per = GROUP * ans
+    for g in range(groups):
+        got = nn(wide_ref[g], weight_ref[:, g * WIDE : (g + 1) * WIDE])
+        for q in range(questions):
+            part = jnp.where(own, got[q * per : (q + 1) * per], 0.0)
+            dest_ref[q * ans : (q + 1) * ans, g * WIDE : (g + 1) * WIDE] = fold(part, ans)
+
+
+def forward_kernel(questions, ans, groups, q_ref, enc_ref, ids_ref, wk_ref, wv_ref,
+                   ctx_ref, p_ref, c_ref, a_ref, bd_ref, stat_ref, m_scr, l_scr):
+    step = pl.program_id(0)
+    per = GROUP * ans
+
+    @pl.when(step == 0)
+    def _():
+        block_diagonal(q_ref, bd_ref, questions, ans, groups)
+        absorb(bd_ref, wk_ref, a_ref, questions, ans, groups)
+
+    scores = nt(a_ref[step], enc_ref[0])
+    scores = scores + jnp.where(ids_ref[0] != 0, 0.0, MASKED)
+    top = jnp.max(scores, axis=1, keepdims=True)
+    probs = jnp.exp(scores - top)
+    total = jnp.sum(probs, axis=1, keepdims=True)
+    low = probs.astype(jnp.bfloat16)
+    p_ref[0] = low
+    wide = nn(low, enc_ref[0]).astype(jnp.bfloat16)
+    for g in range(groups):
+        c_ref[g, pl.ds(pl.multiple_of(step * per, per), per), :] = wide[g * per : (g + 1) * per]
+    m_scr[step] = jnp.broadcast_to(top, m_scr.shape[1:])
+    l_scr[step] = jnp.broadcast_to(total, l_scr.shape[1:])
+
+    @pl.when(step == questions - 1)
+    def _():
+        project_heads(c_ref, wv_ref, ctx_ref, questions, ans, groups)
+        for q in range(questions):
+            stats = jnp.zeros((ans, LANES), jnp.float32)
+            for src, first in ((m_scr, 0), (l_scr, HEAD)):
+                for g in range(groups):
+                    part = jnp.where(own_lane(ans, g, first), src[q, g * per : (g + 1) * per, :], 0.0)
+                    stats = stats + fold(part, ans)
+            stat_ref[q * ans : (q + 1) * ans, :] = stats
+
+
+def whole(shape):
+    return pl.BlockSpec(shape, lambda q: (0,) * len(shape))
+
+
+def per_question(shape):
+    return pl.BlockSpec((1,) + shape, lambda q: (q,) + (0,) * len(shape))
+
+
+def cross_forward(query, encoded, ids, wk, wv, ans):
+    questions, tokens, features = encoded.shape
+    groups = features // WIDE
+    per = GROUP * ans
+    rows = groups * per
+    f32, bf16 = jnp.float32, jnp.bfloat16
+    outs = [
+        ((questions * ans, features), f32),
+        ((questions, rows, tokens), bf16),
+        ((groups, questions * per, features), bf16),
+        ((questions, rows, features), bf16),
+        ((groups, questions * per, WIDE), bf16),
+        ((questions * ans, LANES), f32),
+    ]
+    specs = [whole(s) for s, _ in outs]
+    specs[1] = per_question((rows, tokens))
+    return pl.pallas_call(
+        functools.partial(forward_kernel, questions, ans, groups),
+        grid=(questions,),
+        in_specs=[whole(query.shape), per_question((tokens, features)), per_question((1, tokens)),
+                  whole(wk.shape), whole(wv.shape)],
+        out_specs=specs,
+        out_shape=[jax.ShapeDtypeStruct(s, t) for s, t in outs],
+        scratch_shapes=[pltpu.VMEM((questions, rows, LANES), f32)] * 2,
+        compiler_params=pltpu.CompilerParams(vmem_limit_bytes=48 * 2**20),
+        name="cross_forward",
+    )(query, encoded, ids.reshape(questions, 1, tokens), wk, wv)
+
+
+def backward_kernel(questions, ans, groups, g_ref, w_ref, d_ref, p_ref, enc_ref, wk_ref, wv_ref,
+                    s_ref, wide_ref, b_ref, bd_ref, gq_ref, raw_scr, w_scr, d_scr):
+    step = pl.program_id(0)
+    per = GROUP * ans
+
+    @pl.when(step == 0)
+    def _():
+        block_diagonal(g_ref, bd_ref, questions, ans, groups)
+        for q in range(questions):
+            for src, dst in ((w_ref, w_scr), (d_ref, d_scr)):
+                rows = spread(src[q * ans : (q + 1) * ans, :])
+                for g in range(groups):
+                    part = jnp.sum(jnp.where(own_lane(ans, g), rows, 0.0), axis=1, keepdims=True)
+                    dst[q, g * per : (g + 1) * per, :] = jnp.broadcast_to(part, (per, LANES))
+        for g in range(groups):
+            got = nt(bd_ref[g], wv_ref[:, g * WIDE : (g + 1) * WIDE])
+            for q in range(questions):
+                part = got[q * per : (q + 1) * per]
+                raw_scr[q, g * per : (g + 1) * per, :] = part.astype(jnp.bfloat16)
+                scale = w_scr[q, g * per : (g + 1) * per, :1]
+                b_ref[q, g * per : (g + 1) * per, :] = (part * scale).astype(jnp.bfloat16)
+        for g in range(groups):
+            for q in range(questions):
+                scale = w_scr[q, g * per : (g + 1) * per, :1]
+                part = bd_ref[g, q * per : (q + 1) * per, :].astype(jnp.float32) * scale
+                bd_ref[g, q * per : (q + 1) * per, :] = part.astype(jnp.bfloat16)
+
+    grad_probs = nt(raw_scr[step], enc_ref[0])
+    probs = p_ref[0].astype(jnp.float32) * w_scr[step][:, :1]
+    grad_scores = (probs * (grad_probs - d_scr[step][:, :1])).astype(jnp.bfloat16)
+    s_ref[0] = grad_scores
+    wide = nn(grad_scores, enc_ref[0]).astype(jnp.bfloat16)
+    for g in range(groups):
+        wide_ref[g, pl.ds(pl.multiple_of(step * per, per), per), :] = wide[g * per : (g + 1) * per]
+
+    @pl.when(step == questions - 1)
+    def _():
+        project_heads(wide_ref, wk_ref, gq_ref, questions, ans, groups)
+
+
+def cross_backward(grad_context, weight, delta, probs, encoded, wk, wv, ans):
+    questions, tokens, features = encoded.shape
+    groups = features // WIDE
+    per = GROUP * ans
+    rows = groups * per
+    f32, bf16 = jnp.float32, jnp.bfloat16
+    outs = [
+        ((questions, rows, tokens), bf16),
+        ((groups, questions * per, features), bf16),
+        ((questions, rows, features), bf16),
+        ((groups, questions * per, WIDE), bf16),
+        ((questions * ans, features), f32),
+    ]
+    specs = [per_question((rows, tokens))] + [whole(s) for s, _ in outs[1:]]
+    return pl.pallas_call(
+        functools.partial(backward_kernel, questions, ans, groups),
+        grid=(questions,),
+        in_specs=[whole(grad_context.shape), whole(weight.shape), whole(delta.shape),
+                  per_question((rows, tokens)), per_question((tokens, features)),
+                  whole(wk.shape), whole(wv.shape)],
+        out_specs=specs,
+        out_shape=[jax.ShapeDtypeStruct(s, t) for s, t in outs],
+        scratch_shapes=[pltpu.VMEM((questions, rows, features), bf16),
+                        pltpu.VMEM((questions, rows, LANES), f32),
+                        pltpu.VMEM((questions, rows, LANES), f32)],
+        compiler_params=pltpu.CompilerParams(vmem_limit_bytes=48 * 2**20),
+        name="cross_backward",
+    )(grad_context, weight, delta, probs, encoded, wk, wv)
+
+
+def encoded_kernel(s_ref, p_ref, a_ref, b_ref, out_ref):
+    left = jnp.concatenate([s_ref[0], p_ref[0]], axis=0)
+    right = jnp.concatenate([a_ref[0], b_ref[0]], axis=0)
+    out_ref[0] = tn(left, right).astype(jnp.bfloat16)
+
+
+def encoded_gradient(grad_scores, probs, a, b):
+    questions, rows, tokens = probs.shape
+    features = a.shape[2]
+    return pl.pallas_call(
+        encoded_kernel,
+        grid=(questions,),
+        in_specs=[per_question((rows, tokens))] * 2 + [per_question((rows, features))] * 2,
+        out_specs=per_question((tokens, features)),
+        out_shape=jax.ShapeDtypeStruct((questions, tokens, features), jnp.bfloat16),
+        compiler_params=pltpu.CompilerParams(vmem_limit_bytes=48 * 2**20),
+        name="encoded_gradient",
+    )(grad_scores, probs, a, b)
 
 
 def rms_norm(values, gain_vec):
@@ -62,12 +291,100 @@
     return lax.dynamic_slice_in_dim(values, blk_index * share, share, 1)
 
 
-def combine_stats(earlier, later):
-    maximum = jnp.maximum(earlier[0], later[0])
-    return (
-        maximum,
-        earlier[1] * jnp.exp(earlier[0] - maximum) + later[1] * jnp.exp(later[0] - maximum),
-    )
+def partner(value, axis, bit):
+    count = lax.axis_size(axis)
+    return lax.ppermute(value, axis, [(k, k ^ bit) for k in range(count)])
+
+
+def axis_bits(axis):
+    bits, bit = [], 1
+    while bit < lax.axis_size(axis):
+        bits.append(bit)
+        bit *= 2
+    return bits
+
+
+def halves(value, axis, bit):
+    rows = value.shape[0] // 2
+    mine = (lax.axis_index(axis) // bit) % 2
+    keep = lax.dynamic_slice_in_dim(value, mine * rows, rows, 0)
+    give = lax.dynamic_slice_in_dim(value, (1 - mine) * rows, rows, 0)
+    return keep, give
+
+
+def joined(value, axis, bit):
+    other = partner(value, axis, bit)
+    mine = (lax.axis_index(axis) // bit) % 2
+    first = jnp.where(mine == 0, value, other)
+    second = jnp.where(mine == 0, other, value)
+    return jnp.concatenate([first, second], axis=0)
+
+
+def sum_all(value, axis):
+    bits = axis_bits(axis)
+    keep, give = halves(value, axis, bits[0])
+    keep = keep + partner(give, axis, bits[0])
+    for bit in bits[1:]:
+        keep = keep + partner(keep, axis, bit)
+    return joined(keep, axis, bits[0])
+
+
+def sum_pair(value, axis):
+    for bit in axis_bits(axis):
+        value = value + partner(value, axis, bit)
+    return value
+
+
+def scatter_rows(value, axis):
+    bits = axis_bits(axis)
+    count = lax.axis_size(axis)
+    index = lax.axis_index(axis)
+    rows, width = value.shape
+    value = value.reshape(count, rows // count, width)
+    for bit in bits:
+        mine = (index // bit) % 2
+        left = value.shape[0] // 2
+        pairs = value.reshape(left, 2, rows // count, width)
+        keep = lax.dynamic_index_in_dim(pairs, mine, 1, keepdims=False)
+        give = lax.dynamic_index_in_dim(pairs, 1 - mine, 1, keepdims=False)
+        value = keep + partner(give, axis, bit)
+    return value.reshape(rows // count, width)
+
+
+def merge_kernel(heads, mine_ref, other_ref, out_ref):
+    features = heads * HEAD
+    mine = mine_ref[:, features:]
+    other = other_ref[:, features:]
+    lane = lax.broadcasted_iota(jnp.int32, mine.shape, 1)
+    top_lane = lane < HEAD
+    top_mine = jnp.where(top_lane, mine, pltpu.roll(mine, HEAD, 1))
+    top_other = jnp.where(top_lane, other, pltpu.roll(other, HEAD, 1))
+    top = jnp.maximum(top_mine, top_other)
+    scale_mine = jnp.exp(top_mine - top)
+    scale_other = jnp.exp(top_other - top)
+    out_ref[:, features:] = jnp.where(top_lane, top, mine * scale_mine + other * scale_other)
+    for pair in range(heads // 2):
+        at = slice(pair * LANES, (pair + 1) * LANES)
+        a = jnp.where(top_lane, scale_mine[:, 2 * pair : 2 * pair + 1], scale_mine[:, 2 * pair + 1 : 2 * pair + 2])
+        b = jnp.where(top_lane, scale_other[:, 2 * pair : 2 * pair + 1], scale_other[:, 2 * pair + 1 : 2 * pair + 2])
+        out_ref[:, at] = mine_ref[:, at] * a + other_ref[:, at] * b
+
+
+def merge(mine, other, heads):
+    return pl.pallas_call(
+        functools.partial(merge_kernel, heads),
+        out_shape=jax.ShapeDtypeStruct(mine.shape, mine.dtype),
+        name="merge_partials",
+    )(mine, other)
+
+
+def merge_all(value, axis, heads):
+    bits = axis_bits(axis)
+    keep, give = halves(value, axis, bits[0])
+    keep = merge(keep, partner(give, axis, bits[0]), heads)
+    for bit in bits[1:]:
+        keep = merge(keep, partner(keep, axis, bit), heads)
+    return joined(keep, axis, bits[0])
 
 
 def body(
@@ -93,7 +410,6 @@
 ):
     low_type = jnp.bfloat16
     questions, answer_len, features = decoder_in.shape
-    enc_rows = encoded.shape[1]
     head_count = rel_bias.shape[1]
     head_size = features // head_count
     hidden_units = ffn_in.shape[1]
@@ -132,38 +448,19 @@
     query_cross = (
         matmul(normed_two, cross_q)
         .astype(low_type)
-        .reshape(questions, answer_len, head_count, head_size)
-    )
-    flat_enc = encoded.reshape(questions * enc_rows, features)
-    kv_weights = jnp.concatenate([cross_k, cross_v], axis=1)
-    kv_cross = (
-        matmul(flat_enc, kv_weights)
-        .astype(low_type)
-        .reshape(questions, enc_rows, 2, head_count, head_size)
-    )
-    key_cross = kv_cross[:, :, 0]
-    value_cross = kv_cross[:, :, 1]
-    key_mask = jnp.where(key_ids != 0, 0.0, MASKED)[:, None, None, :]
-
-    def cross_scores():
-        raw_cross = jnp.einsum(
-            "qihd,qjhd->qhij", query_cross, key_cross, preferred_element_type=jnp.float32
-        )
-        return raw_cross + key_mask
-
-    scores = cross_scores()
-    local_top = jnp.max(scores, axis=-1)
-    local_total = jnp.sum(jnp.exp(scores - local_top[..., None]), axis=-1)
-    maximum, normalizer = merged((local_top, local_total), "blk", combine_stats)
-    probs_cross = jnp.exp(scores - maximum[..., None]) / normalizer[..., None]
-    partial_context = jnp.einsum(
-        "qhij,qjhd->qihd",
-        probs_cross.astype(low_type),
-        value_cross,
-        preferred_element_type=jnp.float32,
-    )
-    context_full = lax.psum(partial_context, "blk")
-    context_cross = context_full.reshape(row_count, features)
+    )
+    ctx_part, probs_low, ctx_wide, q_wide, q_blocks, stat_part = cross_forward(
+        query_cross.astype(jnp.float32), encoded, key_ids, cross_k, cross_v, answer_len
+    )
+    merged_all = merge_all(jnp.concatenate([ctx_part, stat_part], axis=1), "blk", head_count)
+    lane = jnp.arange(LANES)
+    spread_heads = (jnp.arange(features)[None, :] // HEAD == lane[:, None]).astype(jnp.float32)
+    top_all = merged_all[:, features : features + HEAD]
+    total_all = merged_all[:, features + HEAD :]
+    per_head = jnp.where(jnp.arange(HEAD) < head_count, 1.0 / total_all, 0.0)
+    weight = jnp.exp(stat_part[:, :HEAD] - top_all) * per_head
+    weight = jnp.concatenate([weight, jnp.zeros_like(weight)], axis=1)
+    context_cross = merged_all[:, :features] * jnp.dot(per_head, spread_heads[:HEAD], precision=HIGHEST)
     after_cross = after_self + exact_mm(context_cross, cross_o)
     norm_three, norm_three_back = jax.vjp(rms_norm, after_cross, gain_ffn)
     normed_three = norm_three.astype(low_type)
@@ -182,40 +479,19 @@
     grad_branch_cross = grad_after_cross.astype(low_type)
     grad_cross_o = exact_tn(columns(context_cross, blk_index, feature_share), grad_branch_cross)
     grad_context_cross = matmul_nt(grad_branch_cross, cross_o).astype(low_type)
-    grad_context_cross = grad_context_cross.reshape(questions, answer_len, head_count, head_size)
-    scores = cross_scores()
-    probs_cross = jnp.exp(scores - maximum[..., None]) / normalizer[..., None]
-    grad_probs = jnp.einsum(
-        "qihd,qjhd->qhij", grad_context_cross, value_cross, preferred_element_type=jnp.float32
-    )
-    delta = lax.psum(jnp.sum(probs_cross * grad_probs, axis=-1), "blk")
-    grad_scores_cross = (probs_cross * (grad_probs - delta[..., None])).astype(low_type)
-    grad_value_cross = jnp.einsum(
-        "qhij,qihd->qjhd",
-        probs_cross.astype(low_type),
-        grad_context_cross,
-        preferred_element_type=jnp.float32,
-    ).astype(low_type)
-    grad_key_cross = jnp.einsum(
-        "qhij,qihd->qjhd", grad_scores_cross, query_cross, preferred_element_type=jnp.float32
-    ).astype(low_type)
-    partial_query = jnp.einsum(
-        "qhij,qjhd->qihd", grad_scores_cross, key_cross, preferred_element_type=jnp.float32
-    )
-    grad_query_cross = lax.psum(partial_query, "blk")
-    grad_query_cross = grad_query_cross.reshape(row_count, features)
-    grad_kv = jnp.concatenate(
-        [
-            grad_key_cross.reshape(questions * enc_rows, features),
-            grad_value_cross.reshape(questions * enc_rows, features),
-        ],
-        axis=1,
-    )
-    grad_encoded = (
-        matmul_nt(grad_kv, kv_weights).reshape(questions, enc_rows, features).astype(low_type)
-    )
-    whole_sum = lax.psum(matmul_tn(flat_enc, grad_kv), "blk")
-    kv_grad_share = lax.dynamic_slice_in_dim(whole_sum, blk_index * feature_share, feature_share, 0)
+    grad_context_cross = grad_context_cross.astype(jnp.float32)
+    delta = lax.dot_general(
+        grad_context_cross * context_cross, spread_heads, (((1,), (1,)), ((), ())), precision=HIGHEST
+    )
+    grad_scores_cross, query_wide, g_wide, g_blocks, partial_query = cross_backward(
+        grad_context_cross, weight, delta, probs_low, encoded, cross_k, cross_v, answer_len
+    )
+    grad_query_cross = sum_all(partial_query, "blk")
+    grad_encoded = encoded_gradient(grad_scores_cross, probs_low, q_wide, g_wide)
+    wide_pairs = jnp.concatenate([query_wide, ctx_wide], axis=0)
+    blocks = jnp.concatenate([q_blocks, g_blocks], axis=0)
+    kv_part = jnp.einsum("grm,grd->mgd", wide_pairs, blocks, preferred_element_type=jnp.float32)
+    kv_grad_share = scatter_rows(kv_part.reshape(features, 2 * features), "blk")
     grad_cross_q = exact_tn(columns(normed_two, blk_index, feature_share), grad_query_cross)
     back_two, grad_gain_cross = norm_two_back(exact_nt(grad_query_cross, cross_q))
     grad_after_self = grad_after_cross + back_two
@@ -245,7 +521,8 @@
     back_one, grad_gain_self = norm_one_back(matmul_nt(grad_qkv, self_weights))
     grad_in = grad_after_self + back_one
     grad_self_qkv = matmul_tn(columns(normed_one, blk_index, feature_share), grad_qkv)
-    summed = lax.psum(
+    summed = jax.tree.map(
+        lambda part: sum_pair(part, "pb"),
         (
             grad_self_qkv,
             grad_self_o,
@@ -259,7 +536,6 @@
             grad_gain_ffn,
             grad_bias,
         ),
-        "pb",
     )
     self_qkv_sum = summed[0]
     kv_sum = summed[3]

time: 800 us -> 310 us (0.39); the launches traced: 785 us -> 307 us
  matrix products: 240 us -> 46 us
  waiting for transfers between devices: 235 us -> 79 us
  blocking collectives: 113 us -> 0 us
  local copies, waits for them, and re-layouts: 151 us -> 59.5 us
  Pallas kernels: 0 us -> 69.3 us
  starting transfers between devices: 0.12 us -> 26.5 us
  between operations: 14.9 us -> 1.76 us
    psum x3 -> x0, waiting for transfers between devices: 235 us -> none  [the longest x1 115 us: body(): grad_query_cross = lax.psum(partial_query, 'blk')]
    dot_general x6 -> x3, matrix products: 111 us -> 6.88 us  [the longest x1 6.04 us: body(): jnp.einsum('grm,grd->mgd', wide_pairs, blocks, preferred_element_type=jnp...]
    ppermute x0 -> x25, waiting for transfers between devices: none -> 79 us  [partner(): return lax.ppermute(value, axis, [(k, k ^ bit) for k in range(count)])]
    pallas_call x0 -> x7, Pallas kernels: none -> 69.3 us  [the longest x1 29.2 us: cross_backward(): pl.pallas_call(functools.partial(backward_kernel, questions, ans, groups)...]
    psum x2 -> x0, blocking collectives: 68 us -> none  [the longest x1 59.1 us: body(): delta = lax.psum(jnp.sum(probs_cross * grad_probs, axis=-1), 'blk')]
    unnamed x146 -> x145, local copies, waits for them, and re-layouts: 68.8 us -> 19.5 us
    all_gather x2 -> x0, blocking collectives: 45 us -> none  [merged(): everything = jax.tree.map(lambda part: lax.all_gather(part, axis), value)]
    convert_element_type x2 -> x0, local copies, waits for them, and re-layouts: 34.3 us -> none  [the longest x1 22 us: body(): grad_key_cross = jnp.einsum('qhij,qihd->qjhd', grad_scores_cross, query_c...]
  transfers between devices with their start and end apart: 3 -> 25, of which waited for: 3 -> 12; matrix products, arithmetic and copies ran while one was open for 6% -> 27% of each run, Pallas kernels for 0% -> 4%
where the time goes in v1:
time: 310 us; the launch traced here: 307 us
  waiting for transfers between devices  79 us (25%)
  Pallas kernels  69.3 us (22%)
  local copies, waits for them, and re-layouts  59.5 us (19%)
  matrix products  46 us (15%)
  starting transfers between devices  26.5 us (9%)
  other arithmetic  25.4 us (8%)
    ppermute x25, waiting for transfers between devices, partner(): return lax.ppermute(value, axis, [(k, k ^ bit) for k in range(count)])  79 us
    pallas_call x1, Pallas kernels, cross_backward(): pl.pallas_call(functools.partial(backward_kernel, questions, ans, groups)...  29.2 us
    ppermute x25, starting transfers between devices, partner(): return lax.ppermute(value, axis, [(k, k ^ bit) for k in range(count)])  26.5 us
    unnamed x145, local copies, waits for them, and re-layouts  19.5 us
    pallas_call x1, Pallas kernels, cross_forward(): pl.pallas_call(functools.partial(forward_kernel, questions, ans, groups),...  18.1 us
    pallas_call x1, Pallas kernels, encoded_gradient(): pl.pallas_call(encoded_kernel, grid=(questions,), in_specs=[per_question(...  13.1 us
    add x11, other arithmetic, sum_pair(): value = value + partner(value, axis, bit)  12.4 us
    dot_general x5, matrix products, matmul(): return jnp.dot(left_side, right_side, preferred_element_type=jnp.float32)  11.8 us
  transfers between devices with their start and end apart: 25, of which 12 were waited for; matrix products, arithmetic and copies ran while one was open for 27% of the time, Pallas kernels for 4%

profile of v1, /device:TPU:0, one launch (start us, length us, event | category | flops | bytes accessed | tf_op | source)
XLA Modules:
  0.0 307.4 jit_solution(13013771203600320526)
XLA Ops:
  8.7 2.1 reshape.198
  10.8 2.8 fusion.90
  14.6 1.8 fusion.93
  17.0 2.0 fusion.22
  23.6 18.1 %cross_forward.1 = (f32[160,768]{1,0:T(8,128)S(1)}, bf16[8,240,1024]{2,1,0:T(8,128)(2,1)}, bf16[3,640,768]{2,1,0:T(8,128)(2,1)}, bf16[8,240,768]{2,1,0:T(8,128)(...) custom-call(f32[160,768]{1,0:T(8,128)S(1)} %fusion.27.q_ref, bf16[8,1024,768]{2,1,0:T(8,128)(2,1)} %enc_ref.3, ...), custom_call_target="tpu_custom_call" | custom-call | tf_op jit(solution)/shard_map/cross_forward/pallas_call | solution.py:147
  45.7 1.8 constant_dynamic-slice_fusion.2
  49.9 2.2 merge_partials.4.mine_ref
  52.1 2.9 collective-permute-start.1
  55.0 7.4 %collective-permute-done.1.other_ref = f32[80,896]{1,0:T(8,128)} collective-permute-done((f32[80,896]{1,0:T(8,128)}, f32[80,896]{1,0:T(8,128)}, u32[]{:S(2)}, u32[]{:S(2)}) %collective-permute-start.1) | collective-permute-done | bytes 286752 | tf_op jit(solution)/shard_map/ppermute | solution.py:296
  62.4 2.2 merge_partials.5.mine_ref
  64.6 1.8 collective-permute-start.2
  66.4 6.9 %collective-permute-done.2.other_ref = f32[80,896]{1,0:T(8,128)} collective-permute-done((f32[80,896]{1,0:T(8,128)}, f32[80,896]{1,0:T(8,128)}, u32[]{:S(2)}, u32[]{:S(2)}) %collective-permute-start.2) | collective-permute-done | bytes 286752 | tf_op jit(solution)/shard_map/ppermute | solution.py:296
  73.3 2.2 merge_partials.6.mine_ref
  75.5 2.5 collective-permute-start.3
  78.0 2.0 copy.124
  80.0 1.9 reshape.201
  81.9 8.4 %collective-permute-done.3.other_ref = f32[80,896]{1,0:T(8,128)} collective-permute-done((f32[80,896]{1,0:T(8,128)}, f32[80,896]{1,0:T(8,128)}, u32[]{:S(2)}, u32[]{:S(2)}) %collective-permute-start.3) | collective-permute-done | bytes 286752 | tf_op jit(solution)/shard_map/ppermute | solution.py:296
  90.3 2.2 merge_partials.7
  92.6 1.7 collective-permute-done.4
  97.9 5.2 %multiply_convert_fusion = (bf16[160,3072]{1,0:T(8,128)(2,1)}, f32[160,3072]{1,0:T(8,128)S(1)}) fusion(bf16[160,768]{1,0:T(8,128)(2,1)S(1)} %multiply_convert_fusion.1, bf16[768,3072]{1,0:T(8,128)(2,1)} %param.35), kind=kOutput, calls=%fused_computation.23 | convolution fusion | flops 759398400 | bytes 7913472 | tf_op jit(solution)/shard_map/dot_general | solution.py:256
  103.2 2.2 fusion.15
  105.4 2.5 multiply_reduce_fusion.1
  109.9 29.2 %cross_backward.1 = (bf16[8,240,1024]{2,1,0:T(8,128)(2,1)}, bf16[3,640,768]{2,1,0:T(8,128)(2,1)}, bf16[8,240,768]{2,1,0:T(8,128)(2,1)}, bf16[3,640,256]{2,1,0:T(8,128)(2,1)S(1)}, f32[160,768]{1,0:T(8,128)S(1)}) custom-call(f32[160,768]{1,0:T(8,128)S(1)} %fusion.26.g_ref, f32[160,128]{1,0:T(8,128)S(1)} %concatenate.24.w_ref, f32[160,128]{1,0:T(8,128)S(1)} %fusion.33.d_ref, ...), custom_call_target="tpu_custom_call" | custom-call | tf_op jit(solution)/shard_map/cross_backward/pallas_call | solution.py:214
  142.5 6.0 %fusion.6 = f32[768,6,256]{0,2,1:T(8,128)} fusion(bf16[3,640,768]{2,1,0:T(8,128)(2,1)S(1)} %copy-done.61, bf16[3,640,768]{2,1,0:T(8,128)(2,1)} %get-tuple-element.37, bf16[3,640,256]{2,1,0:T(8,128)(2,1)S(1)} %get-tuple-element.36, bf16[3,640,256]{2,1,0:T(8,128)(2,1)S(1)} %copy-done.7), kind=kOutput, calls=%fused_computation.12 | convolution fusion | flops 1513881600 | bytes 12582912 | tf_op jit(solution)/shard_map/grm,grd->mgd/dot_general | solution.py:493
  148.5 6.2 %copy.131 = f32[768,6,256]{2,1,0:T(8,128)} copy(f32[768,6,256]{0,2,1:T(8,128)} %fusion.6) | data formatting | bytes 9437184 | tf_op jit(solution)/shard_map/grm,grd->mgd/transpose | solution.py:493
  154.8 7.2 %reshape_reshape_reshape.3 = f32[8,2,48,1536]{3,2,1,0:T(8,128)} reshape(f32[768,6,256]{2,1,0:T(8,128)} %copy.131) | data formatting | bytes 9437184 | tf_op jit(solution)/shard_map/reshape;reshape;reshape | solution.py:347
  162.8 3.3 %dynamic-slice_bitcast_fusion = f32[8,48,1536]{2,1,0:T(8,128)} fusion(f32[8,2,48,1536]{3,2,1,0:T(8,128)} %reshape_reshape_reshape.3, s32[]{:T(128)S(6)} %select_n.150), kind=kLoop, calls=%fused_computation.11 | loop fusion | bytes 4718596 | tf_op jit(solution)/shard_map/jit(dynamic_index_in_dim)/squeeze | solution.py:349
  166.1 3.7 %collective-permute-done.7 = f32[80,768]{1,0:T(8,128)S(1)} collective-permute-done((f32[80,768]{1,0:T(8,128)S(1)}, f32[80,768]{1,0:T(8,128)S(1)}, u32[]{:S(2)}, u32[]{:S(2)}) %collective-permute-start.7) | collective-permute-done | bytes 245792 | tf_op jit(solution)/shard_map/ppermute | solution.py:296
  169.8 2.4 collective-permute-start.8
  174.6 2.0 fusion.51
  176.6 6.2 %collective-permute-done.8 = f32[80,768]{1,0:T(8,128)S(1)} collective-permute-done((f32[80,768]{1,0:T(8,128)S(1)}, f32[80,768]{1,0:T(8,128)S(1)}, u32[]{:S(2)}, u32[]{:S(2)}) %collective-permute-start.8) | collective-permute-done | bytes 245792 | tf_op jit(solution)/shard_map/ppermute | solution.py:296
  184.6 3.9 %collective-permute-done.12 = f32[768]{0:T(1024)S(1)} collective-permute-done((f32[768]{0:T(1024)S(1)}, f32[768]{0:T(1024)S(1)}, u32[]{:S(2)}, u32[]{:S(2)}) %collective-permute-start.12) | collective-permute-done | bytes 3104 | tf_op jit(solution)/shard_map/ppermute | solution.py:296
  188.5 4.1 %convolution_add_fusion.3 = f32[160,768]{1,0:T(8,128)} fusion(f32[160,768]{1,0:T(8,128)S(1)} %copy-done.13, bf16[160,3072]{1,0:T(8,128)(2,1)S(1)} %copy-done.40, bf16[3072,768]{1,0:T(8,128)(2,1)} %param.36), kind=kOutput, calls=%fused_computation.39 | convolution fusion | flops 755097600 | bytes 6684672 | tf_op jit(solution)/shard_map/dot_general | solution.py:256
  194.6 1.8 copy-done.3
  196.4 1.8 copy-done.4
  198.3 13.1 %encoded_gradient.1 = bf16[8,1024,768]{2,1,0:T(8,128)(2,1)} custom-call(bf16[8,240,1024]{2,1,0:T(8,128)(2,1)} %get-tuple-element.32.s_ref, bf16[8,240,1024]{2,1,0:T(8,128)(2,1)} %get-tuple-element.30.p_ref, bf16[8,240,768]{2,1,0:T(8,128)(2,1)S(1)} %copy-done.3, bf16[8,240,768]{2,1,0:T(8,128)(2,1)S(1)} %copy-done.4), custom_call_target="tpu_custom_call" | custom-call | tf_op jit(solution)/shard_map/encoded_gradient/pallas_call | solution.py:239
  212.0 1.7 add.257
  213.6 1.9 add.258
  215.6 2.0 add.260
  218.7 2.0 fusion.40
  221.7 2.1 multiply_reduce_fusion.2
  224.0 2.1 fusion.48
  228.9 2.9 bitcast_add_fusion
  239.0 3.7 %convert_element_type.95 = bf16[160,2304]{1,0:T(8,128)(2,1)} reshape(bf16[8,20,3,12,64]{4,3,2,1,0:T(8,128)(2,1)} %copy.128) | data formatting | bytes 1474560 | tf_op jit(solution)/shard_map/convert_element_type | solution.py:519
  242.7 18.4 %collective-permute-done.18 = f32[4,48,1536]{2,1,0:T(8,128)} collective-permute-done((f32[4,48,1536]{2,1,0:T(8,128)}, f32[4,48,1536]{2,1,0:T(8,128)}, u32[]{:S(2)}, u32[]{:S(2)}) %collective-permute-start.18) | collective-permute-done | bytes 1179680 | tf_op jit(solution)/shard_map/ppermute | solution.py:296
  267.5 3.5 %multiply_reduce_fusion.3 = (f32[768]{0:T(1024)S(1)}, f32[160]{0:T(256)S(1)}, f32[160,768]{1,0:T(8,128)S(1)}) fusion(f32[160,768]{1,0:T(8,128)S(1)} %copy-done.15, f32[160]{0:T(256)S(1)} %rsqrt.30, f32[768]{0:T(1024)S(1)} %copy-done.51, bf16[160,2304]{1,0:T(8,128)(2,1)S(1)} %copy-done.21, bf16[768,2304]{1,0:T(8,128)(2,1)} %copy-done.8), kind=kOutput, calls=%fused_computation.72 | convolution fusion | flops 566967424 | bytes 5266688 | tf_op jit(solution)/shard_map/dot_general | solution.py:260
  271.0 7.1 %collective-permute-done.19 = f32[2,48,1536]{2,1,0:T(8,128)} collective-permute-done((f32[2,48,1536]{2,1,0:T(8,128)}, f32[2,48,1536]{2,1,0:T(8,128)}, u32[]{:S(2)}, u32[]{:S(2)}) %collective-permute-start.19) | collective-permute-done | bytes 589856 | tf_op jit(solution)/shard_map/ppermute | solution.py:296
  281.1 12.5 %collective-permute-done.20 = f32[1,48,1536]{2,1,0:T(8,128)S(1)} collective-permute-done((f32[1,48,1536]{2,1,0:T(8,128)S(1)}, f32[1,48,1536]{2,1,0:T(8,128)S(1)}, u32[]{:S(2)}, u32[]{:S(2)}) %collective-permute-start.20) | collective-permute-done | bytes 294944 | tf_op jit(solution)/shard_map/ppermute | solution.py:296
  (256 shorter events, 71.8 us)
Async XLA Ops:
  0.7 22.6 %copy-start = (bf16[768,768]{1,0:T(8,128)(2,1)S(1)}, bf16[768,768]{1,0:T(8,128)(2,1)}, u32[]{:S(2)}) copy-start(bf16[768,768]{1,0:T(8,128)(2,1)} %param.31) | copy-start | bytes 3538948
  3.3 16.9 %copy-start.14 = (f32[160,768]{1,0:T(8,128)}, f32[160,768]{1,0:T(8,128)S(1)}, u32[]{:S(2)}) copy-start(f32[160,768]{1,0:T(8,128)S(1)} %reshape.197) | copy-start | bytes 1474564
  21.8 20.0 %copy-start.53 = (f32[160]{0:T(256)}, f32[160]{0:T(256)S(1)}, u32[]{:S(2)}) copy-start(f32[160]{0:T(256)S(1)} %fusion.84) | copy-start | bytes 1924
  47.5 1.7 collective-permute-start
  52.1 10.3 %collective-permute-start.1 = (f32[80,896]{1,0:T(8,128)}, f32[80,896]{1,0:T(8,128)}, u32[]{:S(2)}, u32[]{:S(2)}) collective-permute-start(f32[80,896]{1,0:T(8,128)} %merge_partials.4.mine_ref), channel_id=1, source_target_pairs={{0,2},{1,3},{2,0},{3,1},{4,6},{5,7},{6,4},{7,5},{8,10},{9,11},{10,... | collective-permute-start | bytes 860168 | tf_op jit(solution)/shard_map/ppermute | solution.py:296
  64.6 8.7 %collective-permute-start.2 = (f32[80,896]{1,0:T(8,128)}, f32[80,896]{1,0:T(8,128)}, u32[]{:S(2)}, u32[]{:S(2)}) collective-permute-start(f32[80,896]{1,0:T(8,128)} %merge_partials.5.mine_ref), channel_id=1, source_target_pairs={{0,4},{1,5},{2,6},{3,7},{4,0},{5,1},{6,2},{7,3},{8,12},{9,13},{10,... | collective-permute-start | bytes 860168 | tf_op jit(solution)/shard_map/ppermute | solution.py:296
  75.5 14.8 %collective-permute-start.3 = (f32[80,896]{1,0:T(8,128)}, f32[80,896]{1,0:T(8,128)}, u32[]{:S(2)}, u32[]{:S(2)}) collective-permute-start(f32[80,896]{1,0:T(8,128)} %merge_partials.6.mine_ref), channel_id=1, source_target_pairs={{0,8},{1,9},{2,10},{3,11},{4,12},{5,13},{6,14},{7,15},{8,0},{9,1},... | collective-permute-start | bytes 860168 | tf_op jit(solution)/shard_map/ppermute | solution.py:296
  92.5 1.8 collective-permute-start.4
  96.8 12.7 %copy-start.22 = (f32[160,768]{1,0:T(8,128)}, f32[160,768]{1,0:T(8,128)S(1)}, u32[]{:S(2)}) copy-start(f32[160,768]{1,0:T(8,128)S(1)} %fusion.29) | copy-start | bytes 1474564
  96.8 6.4 %slice-start = ((s8[4718592]{0:T(1024)(128)(4,1)}), s8[4194304]{0:T(1024)(128)(4,1)S(1)}, s32[]{:S(2)}) async-start(s8[4718592]{0:T(1024)(128)(4,1)} %bitcast.84), calls=%async_computation | async-start | bytes 8388608
  97.7 10.2 %copy-start.12 = (f32[160,768]{1,0:T(8,128)}, f32[160,768]{1,0:T(8,128)S(1)}, u32[]{:S(2)}) copy-start(f32[160,768]{1,0:T(8,128)S(1)} %get-tuple-element.168) | copy-start | bytes 1474564
  97.9 7.5 %slice-start.2 = ((s8[4718592]{0:T(1024)(128)(4,1)}), s8[4194304]{0:T(1024)(128)(4,1)S(1)}, s32[]{:S(2)}) async-start(s8[4718592]{0:T(1024)(128)(4,1)} %bitcast.86), calls=%async_computation.2 | async-start | bytes 8388608
  109.9 29.4 %copy-start.31 = (bf16[160,3072]{1,0:T(8,128)(2,1)S(1)}, bf16[160,3072]{1,0:T(8,128)(2,1)}, u32[]{:S(2)}) copy-start(bf16[160,3072]{1,0:T(8,128)(2,1)} %copy-done.30) | copy-start | bytes 2949124
  109.9 32.6 %copy-start.61 = (bf16[3,640,768]{2,1,0:T(8,128)(2,1)S(1)}, bf16[3,640,768]{2,1,0:T(8,128)(2,1)}, u32[]{:S(2)}) copy-start(bf16[3,640,768]{2,1,0:T(8,128)(2,1)} %get-tuple-element.38) | copy-start | bytes 8847364
  139.1 1.8 collective-permute-start.5
  139.7 73.9 %collective-permute-start.23 = (f32[48,3072]{1,0:T(8,128)S(1)}, f32[48,3072]{1,0:T(8,128)}, u32[]{:S(2)}, u32[]{:S(2)}) collective-permute-start(f32[48,3072]{1,0:T(8,128)S(1)} %fusion.67), channel_id=1, source_target_pairs={{0,16},{16,0},{1,17},{17,1},{2,18},{18,2},{3,19},{19,3},{4,20},{20... | collective-permute-start | bytes 1769480 | tf_op jit(solution)/shard_map/ppermute | solution.py:296
  140.9 21.0 %collective-permute-start.6 = (f32[80,768]{1,0:T(8,128)S(1)}, f32[80,768]{1,0:T(8,128)S(1)}, u32[]{:S(2)}, u32[]{:S(2)}) collective-permute-start(f32[80,768]{1,0:T(8,128)S(1)} %dynamic-slice_add_fusion), channel_id=1, source_target_pairs={{0,2},{1,3},{2,0},{3,1},{4,6},{5,7},{6,4},{7,5},{8,10},{9,11},{10,... | collective-permute-start | bytes 737288 | tf_op jit(solution)/shard_map/ppermute | solution.py:296
  162.0 10.2 %copy-start.29 = (f32[160,768]{1,0:T(8,128)S(1)}, f32[160,768]{1,0:T(8,128)}, u32[]{:S(2)}) copy-start(f32[160,768]{1,0:T(8,128)} %reshape.201) | copy-start | bytes 1474564
  162.0 10.1 %copy-start.40 = (bf16[160,3072]{1,0:T(8,128)(2,1)S(1)}, bf16[160,3072]{1,0:T(8,128)(2,1)}, u32[]{:S(2)}) copy-start(bf16[160,3072]{1,0:T(8,128)(2,1)} %get-tuple-element.169) | copy-start | bytes 2949124
  162.0 11.5 %copy-start.56 = (f32[768]{0:T(1024)S(1)}, f32[768]{0:T(1024)}, u32[]{:S(2)}) copy-start(f32[768]{0:T(1024)} %get-tuple-element.141) | copy-start | bytes 9220
  162.0 7.7 %collective-permute-start.7 = (f32[80,768]{1,0:T(8,128)S(1)}, f32[80,768]{1,0:T(8,128)S(1)}, u32[]{:S(2)}, u32[]{:S(2)}) collective-permute-start(f32[80,768]{1,0:T(8,128)S(1)} %add.228), channel_id=1, source_target_pairs={{0,4},{1,5},{2,6},{3,7},{4,0},{5,1},{6,2},{7,3},{8,12},{9,13},{10,... | collective-permute-start | bytes 737288 | tf_op jit(solution)/shard_map/ppermute | solution.py:296
  166.1 8.5 %copy-start.17 = (f32[160,768]{1,0:T(8,128)S(1)}, f32[160,768]{1,0:T(8,128)}, u32[]{:S(2)}) copy-start(f32[160,768]{1,0:T(8,128)} %copy-done.16) | copy-start | bytes 1474564
  166.1 22.4 %copy-start.13 = (f32[160,768]{1,0:T(8,128)S(1)}, f32[160,768]{1,0:T(8,128)}, u32[]{:S(2)}) copy-start(f32[160,768]{1,0:T(8,128)} %copy-done.12) | copy-start | bytes 1474564
  166.1 62.8 %collective-permute-start.17 = (f32[8,48,1536]{2,1,0:T(8,128)}, f32[8,48,1536]{2,1,0:T(8,128)}, u32[]{:S(2)}, u32[]{:S(2)}) collective-permute-start(f32[8,48,1536]{2,1,0:T(8,128)} %dynamic-slice_bitcast_fusion), channel_id=1, source_target_pairs={{0,1},{1,0},{2,3},{3,2},{4,5},{5,4},{6,7},{7,6},{8,9},{9,8},{10,11... | collective-permute-start | bytes 7077896 | tf_op jit(solution)/shard_map/ppermute | solution.py:296
  169.8 13.0 %collective-permute-start.8 = (f32[80,768]{1,0:T(8,128)S(1)}, f32[80,768]{1,0:T(8,128)S(1)}, u32[]{:S(2)}, u32[]{:S(2)}) collective-permute-start(f32[80,768]{1,0:T(8,128)S(1)} %add.229), channel_id=1, source_target_pairs={{0,8},{1,9},{2,10},{3,11},{4,12},{5,13},{6,14},{7,15},{8,0},{9,1},... | collective-permute-start | bytes 737288 | tf_op jit(solution)/shard_map/ppermute | solution.py:296
  172.5 43.1 %collective-permute-start.24 = (f32[192,768]{1,0:T(8,128)S(1)}, f32[192,768]{1,0:T(8,128)}, u32[]{:S(2)}, u32[]{:S(2)}) collective-permute-start(f32[192,768]{1,0:T(8,128)S(1)} %fusion.54), channel_id=1, source_target_pairs={{0,16},{16,0},{1,17},{17,1},{2,18},{18,2},{3,19},{19,3},{4,20},{20... | collective-permute-start | bytes 1769480 | tf_op jit(solution)/shard_map/ppermute | solution.py:296
  173.5 15.0 %collective-permute-start.12 = (f32[768]{0:T(1024)S(1)}, f32[768]{0:T(1024)S(1)}, u32[]{:S(2)}, u32[]{:S(2)}) collective-permute-start(f32[768]{0:T(1024)S(1)} %copy-done.56), channel_id=1, source_target_pairs={{0,16},{16,0},{1,17},{17,1},{2,18},{18,2},{3,19},{19,3},{4,20},{20... | collective-permute-start | bytes 9224 | tf_op jit(solution)/shard_map/ppermute | solution.py:296
  182.8 29.2 %collective-permute-start.22 = (f32[48,768]{1,0:T(8,128)}, f32[48,768]{1,0:T(8,128)}, u32[]{:S(2)}, u32[]{:S(2)}) collective-permute-start(f32[48,768]{1,0:T(8,128)} %fusion.51), channel_id=1, source_target_pairs={{0,16},{16,0},{1,17},{17,1},{2,18},{18,2},{3,19},{19,3},{4,20},{20... | collective-permute-start | bytes 442376 | tf_op jit(solution)/shard_map/ppermute | solution.py:296
  188.5 29.1 %collective-permute-start.9 = (f32[80,768]{1,0:T(8,128)}, f32[80,768]{1,0:T(8,128)}, u32[]{:S(2)}, u32[]{:S(2)}) collective-permute-start(f32[80,768]{1,0:T(8,128)} %add.230), channel_id=1, source_target_pairs={{0,1},{1,0},{2,3},{3,2},{4,5},{5,4},{6,7},{7,6},{8,9},{9,8},{10,11... | collective-permute-start | bytes 737288 | tf_op jit(solution)/shard_map/ppermute | solution.py:296
  215.6 6.1 %copy-start.11 = (f32[160,768]{1,0:T(8,128)S(1)}, f32[160,768]{1,0:T(8,128)}, u32[]{:S(2)}) copy-start(f32[160,768]{1,0:T(8,128)} %copy-done.9) | copy-start | bytes 1474564
  215.6 6.1 %copy-start.54 = (f32[160]{0:T(256)S(1)}, f32[160]{0:T(256)}, u32[]{:S(2)}) copy-start(f32[160]{0:T(256)} %copy-done.53) | copy-start | bytes 1924
  217.6 6.2 %copy-start.58 = (f32[160]{0:T(256)S(1)}, f32[160]{0:T(256)}, u32[]{:S(2)}) copy-start(f32[160]{0:T(256)} %copy-done.57) | copy-start | bytes 1924
  220.7 80.6 %collective-permute-start.16 = (f32[48,768]{1,0:T(8,128)}, f32[48,768]{1,0:T(8,128)}, u32[]{:S(2)}, u32[]{:S(2)}) collective-permute-start(f32[48,768]{1,0:T(8,128)} %fusion.40), channel_id=1, source_target_pairs={{0,16},{16,0},{1,17},{17,1},{2,18},{18,2},{3,19},{19,3},{4,20},{20... | collective-permute-start | bytes 442376 | tf_op jit(solution)/shard_map/ppermute | solution.py:296
  226.1 76.8 %collective-permute-start.15 = (f32[48,768]{1,0:T(8,128)}, f32[48,768]{1,0:T(8,128)}, u32[]{:S(2)}, u32[]{:S(2)}) collective-permute-start(f32[48,768]{1,0:T(8,128)} %fusion.48), channel_id=1, source_target_pairs={{0,16},{16,0},{1,17},{17,1},{2,18},{18,2},{3,19},{19,3},{4,20},{20... | collective-permute-start | bytes 442376 | tf_op jit(solution)/shard_map/ppermute | solution.py:296
  233.0 28.1 %collective-permute-start.18 = (f32[4,48,1536]{2,1,0:T(8,128)}, f32[4,48,1536]{2,1,0:T(8,128)}, u32[]{:S(2)}, u32[]{:S(2)}) collective-permute-start(f32[4,48,1536]{2,1,0:T(8,128)} %dynamic-slice_bitcast_fusion.1), channel_id=1, source_target_pairs={{0,2},{1,3},{2,0},{3,1},{4,6},{5,7},{6,4},{7,5},{8,10},{9,11},{10,... | collective-permute-start | bytes 3538952 | tf_op jit(solution)/shard_map/ppermute | solution.py:296
  242.7 22.2 %copy-start.20 = (bf16[160,2304]{1,0:T(8,128)(2,1)S(1)}, bf16[160,2304]{1,0:T(8,128)(2,1)}, u32[]{:S(2)}) copy-start(bf16[160,2304]{1,0:T(8,128)(2,1)} %convert_element_type.95) | copy-start | bytes 2211844
  263.5 14.6 %collective-permute-start.19 = (f32[2,48,1536]{2,1,0:T(8,128)}, f32[2,48,1536]{2,1,0:T(8,128)}, u32[]{:S(2)}, u32[]{:S(2)}) collective-permute-start(f32[2,48,1536]{2,1,0:T(8,128)} %dynamic-slice_bitcast_fusion.2), channel_id=1, source_target_pairs={{0,4},{1,5},{2,6},{3,7},{4,0},{5,1},{6,2},{7,3},{8,12},{9,13},{10,... | collective-permute-start | bytes 1769480 | tf_op jit(solution)/shard_map/ppermute | solution.py:296
  266.1 38.4 %collective-permute-start.14 = (f32[48,2304]{1,0:T(8,128)S(1)}, f32[48,2304]{1,0:T(8,128)}, u32[]{:S(2)}, u32[]{:S(2)}) collective-permute-start(f32[48,2304]{1,0:T(8,128)S(1)} %fusion.71), channel_id=1, source_target_pairs={{0,16},{16,0},{1,17},{17,1},{2,18},{18,2},{3,19},{19,3},{4,20},{20... | collective-permute-start | bytes 1327112 | tf_op jit(solution)/shard_map/ppermute | solution.py:296
  267.4 10.7 %copy-start.27 = (f32[4,48,1536]{2,1,0:T(8,128)S(1)}, f32[4,48,1536]{2,1,0:T(8,128)}, u32[]{:S(2)}) copy-start(f32[4,48,1536]{2,1,0:T(8,128)} %copy-done.26) | copy-start | bytes 3538948
  271.0 8.7 %copy-start.63 = (s32[20,20]{1,0:T(8,128)S(1)}, s32[20,20]{1,0:T(8,128)}, u32[]{:S(2)}) copy-start(s32[20,20]{1,0:T(8,128)} %param.22) | copy-start | bytes 4804
  271.0 10.1 %copy-start.60 = (f32[160]{0:T(256)S(1)}, f32[160]{0:T(256)}, u32[]{:S(2)}) copy-start(f32[160]{0:T(256)} %copy-done.59) | copy-start | bytes 1924
  271.0 22.7 %copy-start.55 = (f32[768]{0:T(1024)S(1)}, f32[768]{0:T(1024)}, u32[]{:S(2)}) copy-start(f32[768]{0:T(1024)} %get-tuple-element.143) | copy-start | bytes 9220
  271.0 27.3 %copy-start.19 = (f32[160,768]{1,0:T(8,128)S(1)}, f32[160,768]{1,0:T(8,128)}, u32[]{:S(2)}) copy-start(f32[160,768]{1,0:T(8,128)} %copy-done.18) | copy-start | bytes 1474564
  279.3 14.4 %collective-permute-start.20 = (f32[1,48,1536]{2,1,0:T(8,128)S(1)}, f32[1,48,1536]{2,1,0:T(8,128)S(1)}, u32[]{:S(2)}, u32[]{:S(2)}) collective-permute-start(f32[1,48,1536]{2,1,0:T(8,128)S(1)} %constant_dynamic-slice_fusion), channel_id=1, source_target_pairs={{0,8},{1,9},{2,10},{3,11},{4,12},{5,13},{6,14},{7,15},{8,0},{9,1},... | collective-permute-start | bytes 884744 | tf_op jit(solution)/shard_map/ppermute | solution.py:296
  280.1 14.7 %collective-permute-start.13 = (f32[32,12]{0,1:T(8,128)S(1)}, f32[32,12]{0,1:T(8,128)S(1)}, u32[]{:S(2)}, u32[]{:S(2)}) collective-permute-start(f32[32,12]{0,1:T(8,128)S(1)} %convolution_bitcast_fusion.1), channel_id=1, source_target_pairs={{0,16},{16,0},{1,17},{17,1},{2,18},{18,2},{3,19},{19,3},{4,20},{20... | collective-permute-start | bytes 4616 | tf_op jit(solution)/shard_map/ppermute | solution.py:296
  293.7 3.6 %collective-permute-start.11 = (f32[768]{0:T(1024)S(1)}, f32[768]{0:T(1024)S(1)}, u32[]{:S(2)}, u32[]{:S(2)}) collective-permute-start(f32[768]{0:T(1024)S(1)} %copy-done.55), channel_id=1, source_target_pairs={{0,16},{16,0},{1,17},{17,1},{2,18},{18,2},{3,19},{19,3},{4,20},{20... | collective-permute-start | bytes 9224 | tf_op jit(solution)/shard_map/ppermute | solution.py:296
  294.7 5.9 %collective-permute-start.10 = (f32[768]{0:T(1024)S(1)}, f32[768]{0:T(1024)S(1)}, u32[]{:S(2)}, u32[]{:S(2)}) collective-permute-start(f32[768]{0:T(1024)S(1)} %get-tuple-element.145), channel_id=1, source_target_pairs={{0,16},{16,0},{1,17},{17,1},{2,18},{18,2},{3,19},{19,3},{4,20},{20... | collective-permute-start | bytes 9224 | tf_op jit(solution)/shard_map/ppermute | solution.py:296
  297.3 9.1 %collective-permute-start.21 = (f32[48,1536]{1,0:T(8,128)S(1)}, f32[48,1536]{1,0:T(8,128)S(1)}, u32[]{:S(2)}, u32[]{:S(2)}) collective-permute-start(f32[48,1536]{1,0:T(8,128)S(1)} %add_bitcast_fusion), channel_id=1, source_target_pairs={{0,16},{16,0},{1,17},{17,1},{2,18},{18,2},{3,19},{19,3},{4,20},{20... | collective-permute-start | bytes 884744 | tf_op jit(solution)/shard_map/ppermute | solution.py:296
  (46 other events, 106.1 us)
